TPU v7x, 32 devices: a whole 2x2x4 slice. The times are simulated.
32 devices in a mesh: dp: 16 (over z, y, x), tensor: 2 (over core).
Axes of the slice: x: 2, y: 2, z: 4, core: 2. Of those that a mesh axis runs over, the one named last changes fastest.
Arguments:
- tokens: float32 [6144, 768], P('dp'), may hold values from -6 to 6
- cotangent: float32 [6144, 768], P('dp'), may hold values from -6 to 6
- doc_ids: int32 [16, 384], P('dp'), may hold values from 0 to 3, never falling along the last dimension, each value on 1 to 288 neighbouring positions
- live_rows: int32 [16], P('dp'), may hold values from 96 to 384, as said below
- ln1_gain: float32 [2, 768], replicated, may hold values from 0.1 to 1.9
- ln1_shift: float32 [2, 768], replicated, may hold values from -3 to 3
- qkv_weight: bfloat16 [2, 3, 768, 768], P(None, None, None, 'tensor'), may hold values from -0.21875 to 0.21875
- qv_bias: float32 [2, 2, 768], P(None, None, 'tensor'), may hold values from -3 to 3
- proj_weight: bfloat16 [2, 768, 768], P(None, 'tensor'), may hold values from -1.75 to 1.75
- proj_bias: float32 [2, 768], replicated, may hold values from -3 to 3
- ln2_gain: float32 [2, 768], replicated, may hold values from 0.1 to 1.9
- ln2_shift: float32 [2, 768], replicated, may hold values from -3 to 3
- fc_weight: bfloat16 [2, 768, 3072], P(None, None, 'tensor'), may hold values from -0.21875 to 0.21875
- fc_bias: float32 [2, 3072], P(None, 'tensor'), may hold values from -3 to 3
- out_weight: bfloat16 [2, 3072, 768], P(None, 'tensor'), may hold values from -0.21875 to 0.21875
- out_bias: float32 [2, 768], replicated, may hold values from -3 to 3
Outputs:
- block_out: float32 [6144, 768], P('dp')
- input_grad: float32 [6144, 768], P('dp')
- grad_ln1_gain: float32 [2, 768], replicated
- grad_ln1_shift: float32 [2, 768], replicated
- grad_qkv: float32 [2, 3, 768, 768], P(None, None, 'dp', 'tensor')
- grad_qv_bias: float32 [2, 2, 768], P(None, None, 'tensor')
- grad_proj: float32 [2, 768, 768], P(None, 'tensor', 'dp')
- grad_proj_bias: float32 [2, 768], replicated
- grad_ln2_gain: float32 [2, 768], replicated
- grad_ln2_shift: float32 [2, 768], replicated
- grad_fc: float32 [2, 768, 3072], P(None, 'dp', 'tensor')
- grad_fc_bias: float32 [2, 3072], P(None, 'tensor')
- grad_out: float32 [2, 3072, 768], P(None, 'tensor', 'dp')
- grad_out_bias: float32 [2, 768], replicated
Inputs may be any that keep to these rules, and one draw needn't show every extreme that they name: `live_rows`: some index of dp has all 384 rows live in every draw; the others hold at least a quarter of them.
All inputs are finite; a program needn't handle non-finite values.
Results may differ from a plain program's by a relative error of at most 0.0003.
Values sent between devices are 32-bit elements; how exact they have to be, the bound alone decides.
No kernel may reach another device: no remote copies, remote signals or barrier semaphores. Data moves between devices by JAX's collectives and lax.ppermute only.
A program may use at most 192 MiB of HBM per device.

v0:
```python
import jax
import jax.numpy as jnp
from jax import lax
from jax.sharding import PartitionSpec as P

HEAD_DIM = 64


EPSILON = 1e-05
HIGHEST = lax.Precision.HIGHEST


def matmul(operand, partner):
    return jnp.dot(operand, partner, precision=HIGHEST, preferred_element_type=jnp.float32)


def rows_contract(operand, partner):
    return lax.dot_general(
        operand,
        partner,
        (((0,), (0,)), ((), ())),
        precision=HIGHEST,
        preferred_element_type=jnp.float32,
    )


def cols_contract(operand, partner):
    return lax.dot_general(
        operand,
        partner,
        (((1,), (1,)), ((), ())),
        precision=HIGHEST,
        preferred_element_type=jnp.float32,
    )


def layer_norm(values, norm_gain, norm_shift):
    row_mean = jnp.mean(values, axis=-1, keepdims=True)
    centred = values - row_mean
    variance = jnp.mean(centred * centred, axis=-1, keepdims=True)
    return centred * lax.rsqrt(variance + EPSILON) * norm_gain + norm_shift


def gelu_tanh(values):
    return jax.nn.gelu(values, approximate=True)


def masked_scores(queries, key_rows, allowed, score_scale):
    scores = jnp.einsum("qhe,khe->hqk", queries, key_rows, precision=HIGHEST) * score_scale
    return jnp.where(allowed[None], scores, jnp.float32(-1e30))


def attend(queries, key_rows, values, allowed, score_scale):
    scores = masked_scores(queries, key_rows, allowed, score_scale)
    row_peak = jnp.max(scores, axis=-1, keepdims=True)
    row_total = jnp.sum(jnp.exp(scores - row_peak), axis=-1, keepdims=True)
    logsum = row_peak + jnp.log(row_total)
    weights = jnp.exp(scores - logsum)
    return (jnp.einsum("hqk,khe->qhe", weights, values, precision=HIGHEST), logsum)


def attend_back(queries, key_rows, values, allowed, score_scale, logsum, result, result_grad):
    weights = jnp.exp(masked_scores(queries, key_rows, allowed, score_scale) - logsum)
    values_grad = jnp.einsum("hqk,qhe->khe", weights, result_grad, precision=HIGHEST)
    weights_grad = jnp.einsum("qhe,khe->hqk", result_grad, values, precision=HIGHEST)
    row_dot = jnp.sum(result_grad * result, axis=-1)
    scores_grad = weights * (weights_grad - jnp.transpose(row_dot)[:, :, None]) * score_scale
    query_grad = jnp.einsum("hqk,khe->qhe", scores_grad, key_rows, precision=HIGHEST)
    key_grad = jnp.einsum("hqk,qhe->khe", scores_grad, queries, precision=HIGHEST)
    return (query_grad, key_grad, values_grad)


def on_device(
    tokens,
    cotangent,
    doc_ids,
    live_rows,
    ln1_gain,
    ln1_shift,
    qkv_weight,
    qv_bias,
    proj_weight,
    proj_bias,
    ln2_gain,
    ln2_shift,
    fc_weight,
    fc_bias,
    out_weight,
    out_bias,
):
    row_count = tokens.shape[0]
    layer_count = qkv_weight.shape[0]
    local_heads = qkv_weight.shape[-1] // HEAD_DIM
    head_shape = (row_count, local_heads, HEAD_DIM)
    score_scale = HEAD_DIM ** (-0.5)
    position = jnp.arange(row_count, dtype=jnp.int32)
    living = position < live_rows[0]
    doc_tags = jnp.where(living, doc_ids[0], -1)
    allowed = (doc_tags[:, None] == doc_tags[None, :]) & (position[None, :] <= position[:, None])
    live_mask = living[:, None].astype(jnp.float32)
    qkv_float = qkv_weight.astype(jnp.float32)
    proj_float = proj_weight.astype(jnp.float32)
    fc_float = fc_weight.astype(jnp.float32)
    out_float = out_weight.astype(jnp.float32)
    stored = []
    stream = tokens
    for number in range(layer_count):
        normed, first_pull = jax.vjp(layer_norm, stream, ln1_gain[number], ln1_shift[number])
        queries = (matmul(normed, qkv_float[number, 0]) + qv_bias[number, 0]).reshape(head_shape)
        key_rows = matmul(normed, qkv_float[number, 1]).reshape(head_shape)
        values = (matmul(normed, qkv_float[number, 2]) + qv_bias[number, 1]).reshape(head_shape)
        attended, logsum = attend(queries, key_rows, values, allowed, score_scale)
        attended_flat = attended.reshape(row_count, -1)
        branch_attn = lax.psum(matmul(attended_flat, proj_float[number]), "tensor")
        middle = stream + branch_attn + proj_bias[number]
        normed_two, second_pull = jax.vjp(layer_norm, middle, ln2_gain[number], ln2_shift[number])
        hidden_in = matmul(normed_two, fc_float[number]) + fc_bias[number]
        activated, gelu_pull = jax.vjp(gelu_tanh, hidden_in)
        branch_mlp = lax.psum(matmul(activated, out_float[number]), "tensor")
        stream = middle + branch_mlp + out_bias[number]
        stored.append(
            (
                first_pull,
                normed,
                queries,
                key_rows,
                values,
                attended,
                attended_flat,
                logsum,
                second_pull,
                normed_two,
                activated,
                gelu_pull,
            )
        )
    block_out = stream * live_mask
    gradient = cotangent * live_mask
    small_terms = [None] * layer_count
    big_terms = [None] * layer_count
    for number in reversed(range(layer_count)):
        (
            first_pull,
            normed,
            queries,
            key_rows,
            values,
            attended,
            attended_flat,
            logsum,
            second_pull,
            normed_two,
            activated,
            gelu_pull,
        ) = stored[number]
        grad_out_bias = jnp.sum(gradient, axis=0)
        grad_out = rows_contract(activated, gradient)
        (hidden_grad,) = gelu_pull(cols_contract(gradient, out_float[number]))
        grad_fc_bias = jnp.sum(hidden_grad, axis=0)
        grad_fc = rows_contract(normed_two, hidden_grad)
        normed_two_grad = lax.psum(cols_contract(hidden_grad, fc_float[number]), "tensor")
        middle_grad, grad_ln2_gain, grad_ln2_shift = second_pull(normed_two_grad)
        gradient = gradient + middle_grad
        grad_proj_bias = jnp.sum(gradient, axis=0)
        grad_proj = rows_contract(attended_flat, gradient)
        attended_grad = cols_contract(gradient, proj_float[number]).reshape(head_shape)
        query_grad, key_grad, values_grad = attend_back(
            queries, key_rows, values, allowed, score_scale, logsum, attended, attended_grad
        )
        query_grad = query_grad.reshape(row_count, -1)
        key_grad = key_grad.reshape(row_count, -1)
        values_grad = values_grad.reshape(row_count, -1)
        grad_qv_bias = jnp.stack([jnp.sum(query_grad, axis=0), jnp.sum(values_grad, axis=0)])
        grad_qkv = jnp.stack(
            [
                rows_contract(normed, query_grad),
                rows_contract(normed, key_grad),
                rows_contract(normed, values_grad),
            ]
        )
        normed_partial = (
            cols_contract(query_grad, qkv_float[number, 0])
            + cols_contract(key_grad, qkv_float[number, 1])
            + cols_contract(values_grad, qkv_float[number, 2])
        )
        normed_grad = lax.psum(normed_partial, "tensor")
        stream_grad, grad_ln1_gain, grad_ln1_shift = first_pull(normed_grad)
        gradient = gradient + stream_grad
        small_terms[number] = (
            grad_ln1_gain,
            grad_ln1_shift,
            grad_qv_bias,
            grad_proj_bias,
            grad_ln2_gain,
            grad_ln2_shift,
            grad_fc_bias,
            grad_out_bias,
        )
        big_terms[number] = (grad_qkv, grad_proj, grad_fc, grad_out)
    stacked_big = [
        jnp.stack([big_terms[number][member] for number in range(layer_count)])
        for member in range(4)
    ]
    fc_view = stacked_big[2].reshape((layer_count, 1) + stacked_big[2].shape[1:])
    qkv_sum, proj_sum, fc_part, out_sum = (
        lax.psum_scatter(stacked_big[0], "dp", scatter_dimension=2, tiled=True),
        lax.psum_scatter(stacked_big[1], "dp", scatter_dimension=2, tiled=True),
        lax.psum_scatter(fc_view, "dp", scatter_dimension=2, tiled=True),
        lax.psum_scatter(stacked_big[3], "dp", scatter_dimension=2, tiled=True),
    )
    fc_sum = fc_part[:, 0]
    stacked_small = [
        jnp.stack([small_terms[number][member] for number in range(layer_count)])
        for member in range(8)
    ]
    (
        ln1_gain_sum,
        ln1_shift_sum,
        qv_bias_sum,
        proj_bias_sum,
        ln2_gain_sum,
        ln2_shift_sum,
        fc_bias_sum,
        out_bias_sum,
    ) = lax.psum(
        (
            stacked_small[0],
            stacked_small[1],
            stacked_small[2],
            stacked_small[3],
            stacked_small[4],
            stacked_small[5],
            stacked_small[6],
            stacked_small[7],
        ),
        "dp",
    )
    return (
        block_out,
        gradient,
        ln1_gain_sum,
        ln1_shift_sum,
        qkv_sum,
        qv_bias_sum,
        proj_sum,
        proj_bias_sum,
        ln2_gain_sum,
        ln2_shift_sum,
        fc_sum,
        fc_bias_sum,
        out_sum,
        out_bias_sum,
    )


def solution(mesh):
    in_specs = (
        P("dp", None),
        P("dp", None),
        P("dp", None),
        P("dp"),
        P(),
        P(),
        P(None, None, None, "tensor"),
        P(None, None, "tensor"),
        P(None, "tensor", None),
        P(),
        P(),
        P(),
        P(None, None, "tensor"),
        P(None, "tensor"),
        P(None, "tensor", None),
        P(),
    )
    out_specs = (
        P("dp", None),
        P("dp", None),
        P(),
        P(),
        P(None, None, "dp", "tensor"),
        P(None, None, "tensor"),
        P(None, "tensor", "dp"),
        P(),
        P(),
        P(),
        P(None, "dp", "tensor"),
        P(None, "tensor"),
        P(None, "tensor", "dp"),
        P(),
    )
    return jax.shard_map(
        on_device, mesh=mesh, in_specs=in_specs, out_specs=out_specs, check_vma=False
    )
```

profile of v0, /device:TPU:0, one launch (start us, length us, event | category | flops | bytes accessed | tf_op | source)
XLA Modules:
  0.0 1026.1 jit_solution(12739262963104154814)
XLA Ops:
  37.1 20.2 %all-reduce.14.cloned.1.call-done = f32[384,768]{1,0:T(8,128)} async-done(((f32[384,768]{1,0:T(8,128)}), f32[384,768]{1,0:T(8,128)}) %all-reduce.14.cloned.1.call-update) | async-done | bytes 1179664 | tf_op jit(solution)/shard_map/psum | solution.py:114
  59.1 5.3 convolution_add_fusion.1
  65.9 4.9 fusion.23
  73.0 19.0 %all-reduce.16.cloned.1.call-done = f32[384,768]{1,0:T(8,128)} async-done(((f32[384,768]{1,0:T(8,128)}), f32[384,768]{1,0:T(8,128)}) %all-reduce.16.cloned.1.call-update) | async-done | bytes 1179664 | tf_op jit(solution)/shard_map/psum | solution.py:119
  112.0 20.5 %all-reduce.18.cloned.1.call-done = f32[384,768]{1,0:T(8,128)} async-done(((f32[384,768]{1,0:T(8,128)}), f32[384,768]{1,0:T(8,128)}) %all-reduce.18.cloned.1.call-update) | async-done | bytes 1179664 | tf_op jit(solution)/shard_map/psum | solution.py:114
  139.9 7.0 fusion.165
  155.0 18.5 %all-reduce.20.cloned.1.call-done = f32[384,768]{1,0:T(8,128)} async-done(((f32[384,768]{1,0:T(8,128)}), f32[384,768]{1,0:T(8,128)}) %all-reduce.20.cloned.1.call-update) | async-done | bytes 1179664 | tf_op jit(solution)/shard_map/psum | solution.py:161
  190.9 5.3 bitcast_reduce_fusion.2
  202.3 20.9 %all-reduce.22.cloned.1.call-done = f32[384,768]{1,0:T(8,128)} async-done(((f32[384,768]{1,0:T(8,128)}), f32[384,768]{1,0:T(8,128)}) %all-reduce.22.cloned.1.call-update) | async-done | bytes 1179664 | tf_op jit(solution)/shard_map/psum | solution.py:186
  228.6 7.1 fusion.166
  241.6 7.1 fusion.16
  248.7 13.8 %all-reduce.24.cloned.1.call-done = f32[384,768]{1,0:T(8,128)} async-done(((f32[384,768]{1,0:T(8,128)}), f32[384,768]{1,0:T(8,128)}) %all-reduce.24.cloned.1.call-update) | async-done | bytes 1179664 | tf_op jit(solution)/shard_map/psum | solution.py:161
  280.7 4.9 bitcast_reduce_fusion
  291.8 11.8 %convolution_bitcast_fusion = f32[1,1536,768]{2,1,0:T(8,128)S(1)} fusion(f32[384,1536]{1,0:T(8,128)} %copy-done.140, f32[384,768]{1,0:T(8,128)} %param.17, f32[384]{0:T(512)} %fusion.121), kind=kOutput, calls=%fused_computation.3 | convolution fusion | flops 5440831488 | bytes 8259072 | tf_op jit(solution)/shard_map/dot_general | solution.py:18
  306.7 9.2 convolution_bitcast_fusion.1
  320.2 14.9 %copy.57 = f32[2,1536,768]{1,0,2:T(2,128)} copy(f32[2,1536,768]{2,1,0:T(8,128)} %pad_maximum_fusion) | data formatting | bytes 18874368 | tf_op jit(solution)/shard_map/stack | solution.py:201
  340.4 5.3 copy.56
  346.2 5.2 convolution_bitcast_fusion.6
  376.9 10.2 convolution_bitcast_fusion.2
  387.2 8.6 convolution_bitcast_fusion.3
  411.2 81.8 %all-reduce.2 = (f32[2,768]{1,0:T(2,128)}, f32[2,768]{1,0:T(2,128)}, f32[2,2,384]{2,1,0:T(2,128)}, f32[2,768]{1,0:T(2,128)}, f32[2,768]{1,0:T(2,128)}, /*index=5...) all-reduce(f32[2,768]{1,0:T(2,128)} %pad_maximum_fusion.4, ...), channel_id=1, replica_groups=mesh['dp'=16,'tensor'=2] {'dp'}, use_global_device_ids=true, to_apply=%region_32.33 | all-reduce | flops 13824 | bytes 110592 | tf_op jit(solution)/shard_map/psum | solution.py:225
  497.8 189.5 %all-reduce.26.cloned.1.call-done = (f32[2,384,768]{1,0,2:T(2,128)}, f32[2,1536,768]{1,0,2:T(2,128)}) async-done(((f32[2,384,768]{1,0,2:T(2,128)}, f32[2,1536,768]{1,0,2:T(2,128)}), (f32[2,384,768]{1,0,2:T(2,128)}, f32[2,1536,768]{1,0,2:T(2,128)})) %all-reduce.26.cloned.1.call-update) | async-done | bytes 11796496
  691.0 151.8 %reduce-scatter.3.cloned.1.call-done = f32[2,3,48,384]{3,2,1,0:T(8,128)} async-done(((f32[2,3,768,384]{3,2,1,0:T(8,128)}), f32[2,3,48,384]{3,2,1,0:T(8,128)}) %reduce-scatter.3.cloned.1.call-update) | async-done | bytes 442384 | tf_op jit(solution)/shard_map/reduce_scatter | solution.py:206
  842.8 176.1 %reduce-scatter.5.cloned.1.call-done = f32[2,1,48,1536]{3,2,0,1:T(8,128)} async-done(((f32[2,1,768,1536]{3,2,0,1:T(8,128)}), f32[2,1,48,1536]{3,2,0,1:T(8,128)}) %reduce-scatter.5.cloned.1.call-update) | async-done | bytes 589840 | tf_op jit(solution)/shard_map/reduce_scatter | solution.py:208
  (448 shorter events, 189.4 us)
Async XLA Ops:
  7.2 50.0 %all-reduce.14.cloned.1.call-start = ((), (), s32[]{:S(2)}) async-start(), calls=%async_computation.2 | async-start | bytes 2359296 | tf_op jit(solution)/shard_map/psum | solution.py:114
  10.4 11.0 %copy-start.67 = (f32[384]{0:T(512)}, f32[384]{0:T(512)S(1)}, u32[]{:S(2)}) copy-start(f32[384]{0:T(512)S(1)} %fusion.123) | copy-start | bytes 4612
  16.3 11.9 %copy-start.44 = (f32[384,384]{0,1:T(8,128)}, f32[384,384]{0,1:T(8,128)S(1)}, u32[]{:S(2)}) copy-start(f32[384,384]{0,1:T(8,128)S(1)} %convolution_add_fusion.9) | copy-start | bytes 1769476
  34.6 57.4 %all-reduce.16.cloned.1.call-start = ((), (), s32[]{:S(2)}) async-start(), calls=%async_computation.3 | async-start | bytes 2359296 | tf_op jit(solution)/shard_map/psum | solution.py:119
  37.1 22.0 %copy-start.75 = (f32[768]{0:T(1024)}, f32[768]{0:T(1024)S(1)}, u32[]{:S(2)}) copy-start(f32[768]{0:T(1024)S(1)} %get-tuple-element.133) | copy-start | bytes 9220
  37.1 22.0 %copy-start.125 = (f32[768]{0:T(1024)}, f32[768]{0:T(1024)S(1)}, u32[]{:S(2)}) copy-start(f32[768]{0:T(1024)S(1)} %get-tuple-element.61) | copy-start | bytes 9220
  58.7 33.3 %copy-start.5 = (f32[384,768]{1,0:T(8,128)}, f32[384,768]{1,0:T(8,128)S(1)}, u32[]{:S(2)}) copy-start(f32[384,768]{1,0:T(8,128)S(1)} %get-tuple-element.105) | copy-start | bytes 3538948
  70.8 61.7 %all-reduce.18.cloned.1.call-start = ((), (), s32[]{:S(2)}) async-start(), calls=%async_computation.4 | async-start | bytes 2359296 | tf_op jit(solution)/shard_map/psum | solution.py:114
  111.4 62.1 %all-reduce.20.cloned.1.call-start = ((), (), s32[]{:S(2)}) async-start(), calls=%async_computation.5 | async-start | bytes 2359296 | tf_op jit(solution)/shard_map/psum | solution.py:161
  134.9 13.3 %slice-start = ((s8[4718592]{0:T(1024)(128)(4,1)}), s8[4194304]{0:T(1024)(128)(4,1)S(1)}, s32[]{:S(2)}) async-start(s8[4718592]{0:T(1024)(128)(4,1)} %bitcast.244), calls=%async_computation.12 | async-start | bytes 8388608
  152.4 70.9 %all-reduce.22.cloned.1.call-start = ((), (), s32[]{:S(2)}) async-start(), calls=%async_computation.6 | async-start | bytes 2359296 | tf_op jit(solution)/shard_map/psum | solution.py:186
  202.1 60.4 %all-reduce.24.cloned.1.call-start = ((), (), s32[]{:S(2)}) async-start(), calls=%async_computation.7 | async-start | bytes 2359296 | tf_op jit(solution)/shard_map/psum | solution.py:161
  241.4 166.2 %all-reduce.28.cloned.1.call-start = ((), (), s32[]{:S(2)}) async-start(), calls=%async_computation.11 | async-start | bytes 4718592 | tf_op jit(solution)/shard_map/psum | solution.py:119
  291.5 395.8 %all-reduce.26.cloned.1.call-start = ((), (), s32[]{:S(2)}) async-start(), calls=%async_computation.10 | async-start | bytes 23592960
  291.7 11.9 %copy-start.12 = (f32[384,768]{1,0:T(8,128)S(1)}, f32[384,768]{1,0:T(8,128)}, u32[]{:S(2)}) copy-start(f32[384,768]{1,0:T(8,128)} %copy-done.10) | copy-start | bytes 3538948
  291.8 11.9 %copy-start.21 = (f32[6,64,384]{2,1,0:T(8,128)S(1)}, f32[6,64,384]{2,1,0:T(8,128)}, u32[]{:S(2)}) copy-start(f32[6,64,384]{2,1,0:T(8,128)} %copy-done.19) | copy-start | bytes 1769476
  291.8 15.0 %copy-start.139 = (f32[384,1536]{1,0:T(8,128)S(1)}, f32[384,1536]{1,0:T(8,128)}, u32[]{:S(2)}) copy-start(f32[384,1536]{1,0:T(8,128)} %copy-done.137) | copy-start | bytes 7077892
  345.7 497.1 %reduce-scatter.3.cloned.1.call-start = ((), (), s32[]{:S(2)}) async-start(), calls=%async_computation.8 | async-start | bytes 7520256 | tf_op jit(solution)/shard_map/reduce_scatter | solution.py:206
  376.8 10.3 %copy-start.7 = (f32[384,768]{1,0:T(8,128)S(1)}, f32[384,768]{1,0:T(8,128)}, u32[]{:S(2)}) copy-start(f32[384,768]{1,0:T(8,128)} %copy-done.5) | copy-start | bytes 3538948
  376.8 10.3 %copy-start.77 = (f32[768]{0:T(1024)S(1)}, f32[768]{0:T(1024)}, u32[]{:S(2)}) copy-start(f32[768]{0:T(1024)} %copy-done.75) | copy-start | bytes 9220
  376.8 642.0 %reduce-scatter.5.cloned.1.call-start = ((), (), s32[]{:S(2)}) async-start(), calls=%async_computation.9 | async-start | bytes 10027008 | tf_op jit(solution)/shard_map/reduce_scatter | solution.py:208
  376.9 10.2 copy-start.82
  407.5 85.5 %copy-start.89 = (f32[384]{0:T(512)S(1)}, f32[384]{0:T(512)}, u32[]{:S(2)}) copy-start(f32[384]{0:T(512)} %copy-done.88) | copy-start | bytes 4612
  407.5 86.2 %copy-start.34 = (f32[384,768]{1,0:T(8,128)S(1)}, f32[384,768]{1,0:T(8,128)}, u32[]{:S(2)}) copy-start(f32[384,768]{1,0:T(8,128)} %get-tuple-element.85) | copy-start | bytes 3538948
  (133 other events, 438.6 us)
Sparse Core Ops, SparseCore 0:
  34.7 22.4 all-reduce.13
  71.0 20.9 all-reduce.15
  111.5 20.9 all-reduce.17
  152.5 20.9 all-reduce.19
  202.2 20.9 all-reduce.21
  241.5 20.9 all-reduce.23
  291.6 22.8 all-reduce.27
  345.8 341.4 all-reduce.25
  693.2 149.4 reduce-scatter.2
  848.9 169.9 reduce-scatter.4
where the time goes:
time: 1040 us; the launch traced here: 1030 us
  waiting for transfers between devices  630 us (61%)
  matrix products  195 us (19%)
  blocking collectives  81.8 us (8%)
  local copies, waits for them, and re-layouts  52.1 us (5%)
  other arithmetic  47.4 us (5%)
  between operations  17.7 us (2%)
    unnamed x11, waiting for transfers between devices  190 us
    reduce_scatter x1, waiting for transfers between devices, on_device(): lax.psum_scatter(fc_view, 'dp', scatter_dimension=2, tiled=True)  176 us
    reduce_scatter x1, waiting for transfers between devices, on_device(): lax.psum_scatter(stacked_big[0], 'dp', scatter_dimension=2, tiled=True)  152 us
    psum x1, blocking collectives, on_device(): lax.psum((stacked_small[0], stacked_small[1], stacked_small[2], stacked_s...  81.8 us
    dot_general x12, matrix products, rows_contract(): lax.dot_general(operand, partner, (((0,), (0,)), ((), ())), precision=HIG...  72.4 us
    dot_general x12, matrix products, matmul(): jnp.dot(operand, partner, precision=HIGHEST, preferred_element_type=jnp.f...  40.8 us
    psum x2, waiting for transfers between devices, on_device(): branch_attn = lax.psum(matmul(attended_flat, proj_float[number]), 'tensor')  40.7 us
    dot_general x12, matrix products, cols_contract(): lax.dot_general(operand, partner, (((1,), (1,)), ((), ())), precision=HIG...  36.3 us
  transfers between devices with their start and end apart: 10, of which 9 were waited for; matrix products, arithmetic and copies ran while one was open for 13% of the time, Pallas kernels for 0%

commit v1 on v0

v1 whole, which is shorter than its diff:
```python
import functools

import jax
import jax.numpy as jnp
from jax import lax
from jax.experimental import pallas as pl
from jax.experimental.pallas import tpu as pltpu
from jax.sharding import PartitionSpec as P

HEAD_DIM = 64
EPSILON = 1e-05
HIGH = lax.Precision.HIGH
LANES = 128
F32 = jnp.float32
BF16 = jnp.bfloat16


def split_two(values):
    high = lax.reduce_precision(values, 8, 7)
    return high.astype(BF16), (values - high).astype(BF16)


def weight_product(values, weight, contract):
    high, low = split_two(values)
    dims = (((1,), (contract,)), ((), ()))
    first = lax.dot_general(high, weight, dims, preferred_element_type=F32)
    return first + lax.dot_general(low, weight, dims, preferred_element_type=F32)


def pair_sum(values, pairs):
    return values + lax.ppermute(values, "tensor", pairs)


def norm_forward(values, norm_gain, norm_shift):
    centred = values - jnp.mean(values, axis=-1, keepdims=True)
    scale = lax.rsqrt(jnp.mean(centred * centred, axis=-1, keepdims=True) + EPSILON)
    unit = centred * scale
    return unit * norm_gain + norm_shift, unit, scale


def norm_backward(grad, unit, scale, norm_gain):
    gained = grad * norm_gain
    mean_grad = jnp.mean(gained, axis=-1, keepdims=True)
    mean_dot = jnp.mean(gained * unit, axis=-1, keepdims=True)
    return (
        scale * (gained - mean_grad - unit * mean_dot),
        jnp.sum(grad * unit, axis=0),
        jnp.sum(grad, axis=0),
    )


GELU_A = 0.7978845608028654
GELU_B = 0.044715


def gelu_forward(values):
    bent = jnp.tanh(GELU_A * (values + GELU_B * values * values * values))
    return 0.5 * values * (1.0 + bent)


def gelu_slope(values):
    square = values * values
    bent = jnp.tanh(GELU_A * (values + GELU_B * values * square))
    inner = GELU_A * (1.0 + 3.0 * GELU_B * square)
    return 0.5 * (1.0 + bent) + 0.5 * values * (1.0 - bent * bent) * inner


def masked_scores(queries, key_rows, allowed, score_scale):
    scores = jnp.einsum("qhe,khe->hqk", queries, key_rows, precision=HIGH) * score_scale
    return jnp.where(allowed[None], scores, jnp.float32(-1e30))


def attend(queries, key_rows, values, allowed, score_scale):
    scores = masked_scores(queries, key_rows, allowed, score_scale)
    row_peak = jnp.max(scores, axis=-1, keepdims=True)
    row_total = jnp.sum(jnp.exp(scores - row_peak), axis=-1, keepdims=True)
    logsum = row_peak + jnp.log(row_total)
    weights = jnp.exp(scores - logsum)
    return jnp.einsum("hqk,khe->qhe", weights, values, precision=HIGH), logsum


def attend_back(queries, key_rows, values, allowed, score_scale, logsum, result, result_grad):
    weights = jnp.exp(masked_scores(queries, key_rows, allowed, score_scale) - logsum)
    values_grad = jnp.einsum("hqk,qhe->khe", weights, result_grad, precision=HIGH)
    weights_grad = jnp.einsum("qhe,khe->hqk", result_grad, values, precision=HIGH)
    row_dot = jnp.sum(result_grad * result, axis=-1)
    scores_grad = weights * (weights_grad - jnp.transpose(row_dot)[:, :, None]) * score_scale
    query_grad = jnp.einsum("hqk,khe->qhe", scores_grad, key_rows, precision=HIGH)
    key_grad = jnp.einsum("hqk,qhe->khe", scores_grad, queries, precision=HIGH)
    return query_grad, key_grad, values_grad


def bit_orders(count):
    bits = [1 << at for at in range(count.bit_length() - 1)]
    lead, rest = bits[:3], bits[3:]
    return [lead[at:] + lead[:at] + rest for at in range(len(lead))]


def block_masks(order):
    masks = [0]
    for bit in reversed(order):
        masks = masks + [mask + bit for mask in masks]
    return masks


def grad_kernel(orders, widths, permuted, me_ref, a_ref, b_ref, *refs):
    outs = refs[: 2 * len(orders)]
    turned_high, turned_low, high_ref, low_ref = refs[2 * len(orders):]
    depth = high_ref.shape[0]
    half = depth // 2
    if not permuted:
        turned = a_ref[...].T
        high = turned.astype(BF16)
        turned_high[...] = high
        turned_low[...] = (turned - high.astype(F32)).astype(BF16)
    start = 0
    for number, order in enumerate(orders):
        masks = block_masks(order)
        if permuted:
            turned = a_ref[number]
            high = turned.astype(BF16)
            high_ref[...] = high
            low_ref[...] = (turned - high.astype(F32)).astype(BF16)
        else:
            rows = depth // len(masks)
            for place, mask in enumerate(masks):
                source = pl.ds(pl.multiple_of((me_ref[0] ^ mask) * rows, 16), rows)
                target = pl.ds(place * rows, rows)
                high_ref[target, :] = turned_high[source, :]
                low_ref[target, :] = turned_low[source, :]
        part = b_ref[:, start:start + widths[number]]
        part_high = part.astype(BF16)
        part_low = (part - part_high.astype(F32)).astype(BF16)
        for which in (1, 0):
            rows_at = pl.ds(which * half, half)
            out_ref = outs[2 * number + 1 - which]
            out_ref[...] = (
                jnp.dot(high_ref[rows_at, :], part_high, preferred_element_type=F32)
                + jnp.dot(high_ref[rows_at, :], part_low, preferred_element_type=F32)
                + jnp.dot(low_ref[rows_at, :], part_high, preferred_element_type=F32)
            )
        start += widths[number]


def grad_parts(left, right, me, count):
    orders = bit_orders(count)
    depth, columns = left.shape[1], right.shape[1]
    widths = flow_widths(columns)
    rows = depth // count
    permuted = rows % 16 != 0
    if permuted:
        blocks = left.T.reshape(count, rows, left.shape[0])
        left = jnp.stack(
            [
                jnp.take(blocks, me ^ jnp.array(block_masks(order), jnp.int32), axis=0).reshape(depth, -1)
                for order in orders
            ]
        )
    tokens = right.shape[0]
    shapes = []
    for width in widths:
        shapes += [jax.ShapeDtypeStruct((depth // 2, width), F32)] * 2
    outs = pl.pallas_call(
        functools.partial(grad_kernel, orders, widths, permuted),
        out_shape=shapes,
        in_specs=[pl.BlockSpec(memory_space=pltpu.SMEM)] + [pl.BlockSpec(memory_space=pltpu.VMEM)] * 2,
        out_specs=[pl.BlockSpec(memory_space=pltpu.VMEM)] * len(shapes),
        scratch_shapes=[pltpu.VMEM((depth, tokens), BF16)] * 4,
        compiler_params=pltpu.CompilerParams(vmem_limit_bytes=40 * 2**20),
        cost_estimate=pl.CostEstimate(
            flops=6 * depth * tokens * columns,
            bytes_accessed=4 * (depth * tokens + tokens * columns + depth * columns),
            transcendentals=0,
        ),
    )(me.reshape(1), left, right)
    return [(outs[2 * at], outs[2 * at + 1]) for at in range(len(orders))]


def flow_widths(columns):
    tiles = columns // LANES
    return {
        12: (6 * LANES, 4 * LANES, 2 * LANES),
        9: (4 * LANES, 3 * LANES, 2 * LANES),
        3: (LANES, LANES, LANES),
    }[tiles]


def scatter(parts, count):
    orders = bit_orders(count)
    done = []
    for (send, keep), order in zip(parts, orders):
        for at, bit in enumerate(order):
            got = lax.ppermute(send, "dp", [(one, one ^ bit) for one in range(count)])
            if at + 1 < len(order):
                half = keep.shape[0] // 2
                send = keep[half:] + got[half:]
                keep = keep[:half] + got[:half]
            else:
                keep = keep + got
        done.append(keep)
    return jnp.concatenate(done, axis=1)


def small_sum(values, count):
    bit = 1
    while bit < count:
        values = values + lax.ppermute(values, "dp", [(one, one ^ bit) for one in range(count)])
        bit *= 2
    return values


def on_device(
    count,
    pair,
    tokens,
    cotangent,
    doc_ids,
    live_rows,
    ln1_gain,
    ln1_shift,
    qkv_weight,
    qv_bias,
    proj_weight,
    proj_bias,
    ln2_gain,
    ln2_shift,
    fc_weight,
    fc_bias,
    out_weight,
    out_bias,
):
    row_count = tokens.shape[0]
    layer_count = qkv_weight.shape[0]
    local_heads = qkv_weight.shape[-1] // HEAD_DIM
    head_shape = (row_count, local_heads, HEAD_DIM)
    score_scale = HEAD_DIM ** (-0.5)
    pairs = [(one, one ^ 1) for one in range(pair)]
    me = lax.axis_index("dp").astype(jnp.int32)
    position = jnp.arange(row_count, dtype=jnp.int32)
    living = position < live_rows[0]
    doc_tags = jnp.where(living, doc_ids[0], -1)
    allowed = (doc_tags[:, None] == doc_tags[None, :]) & (position[None, :] <= position[:, None])
    live_mask = living[:, None].astype(F32)
    stored = []
    stream = tokens
    for number in range(layer_count):
        normed, unit, scale = norm_forward(stream, ln1_gain[number], ln1_shift[number])
        queries = (weight_product(normed, qkv_weight[number, 0], 0) + qv_bias[number, 0]).reshape(head_shape)
        key_rows = weight_product(normed, qkv_weight[number, 1], 0).reshape(head_shape)
        values = (weight_product(normed, qkv_weight[number, 2], 0) + qv_bias[number, 1]).reshape(head_shape)
        attended, logsum = attend(queries, key_rows, values, allowed, score_scale)
        attended_flat = attended.reshape(row_count, -1)
        branch = pair_sum(weight_product(attended_flat, proj_weight[number], 0), pairs)
        middle = stream + branch + proj_bias[number]
        normed_two, unit_two, scale_two = norm_forward(middle, ln2_gain[number], ln2_shift[number])
        hidden_in = weight_product(normed_two, fc_weight[number], 0) + fc_bias[number]
        activated = gelu_forward(hidden_in)
        branch = pair_sum(weight_product(activated, out_weight[number], 0), pairs)
        stream = middle + branch + out_bias[number]
        stored.append(
            (normed, unit, scale, queries, key_rows, values, attended, logsum, normed_two, unit_two, scale_two, hidden_in, activated)
        )
    block_out = stream * live_mask
    gradient = cotangent * live_mask
    small_terms = [None] * layer_count
    big_terms = [None] * layer_count
    for number in reversed(range(layer_count)):
        (normed, unit, scale, queries, key_rows, values, attended, logsum, normed_two, unit_two, scale_two, hidden_in, activated) = stored[number]
        attended_flat = attended.reshape(row_count, -1)
        grad_out_bias = jnp.sum(gradient, axis=0)
        grad_out = scatter(grad_parts(gradient, activated, me, count), count)
        hidden_grad = gelu_slope(hidden_in) * weight_product(gradient, out_weight[number], 1)
        grad_fc_bias = jnp.sum(hidden_grad, axis=0)
        grad_fc = scatter(grad_parts(normed_two, hidden_grad, me, count), count)
        normed_two_grad = pair_sum(weight_product(hidden_grad, fc_weight[number], 1), pairs)
        middle_grad, grad_ln2_gain, grad_ln2_shift = norm_backward(normed_two_grad, unit_two, scale_two, ln2_gain[number])
        gradient = gradient + middle_grad
        grad_proj_bias = jnp.sum(gradient, axis=0)
        grad_proj = scatter(grad_parts(gradient, attended_flat, me, count), count)
        attended_grad = weight_product(gradient, proj_weight[number], 1).reshape(head_shape)
        query_grad, key_grad, values_grad = attend_back(
            queries, key_rows, values, allowed, score_scale, logsum, attended, attended_grad
        )
        query_grad = query_grad.reshape(row_count, -1)
        key_grad = key_grad.reshape(row_count, -1)
        values_grad = values_grad.reshape(row_count, -1)
        grad_qv_bias = jnp.concatenate([jnp.sum(query_grad, axis=0), jnp.sum(values_grad, axis=0)])
        joined = jnp.concatenate([query_grad, key_grad, values_grad], axis=1)
        grad_qkv = scatter(grad_parts(normed, joined, me, count), count)
        normed_partial = (
            weight_product(query_grad, qkv_weight[number, 0], 1)
            + weight_product(key_grad, qkv_weight[number, 1], 1)
            + weight_product(values_grad, qkv_weight[number, 2], 1)
        )
        normed_grad = pair_sum(normed_partial, pairs)
        stream_grad, grad_ln1_gain, grad_ln1_shift = norm_backward(normed_grad, unit, scale, ln1_gain[number])
        gradient = gradient + stream_grad
        small_terms[number] = (
            grad_ln1_gain,
            grad_ln1_shift,
            grad_qv_bias,
            grad_proj_bias,
            grad_ln2_gain,
            grad_ln2_shift,
            grad_fc_bias,
            grad_out_bias,
        )
        big_terms[number] = (grad_qkv, grad_proj, grad_fc, grad_out)
    flat_small = jnp.concatenate([term for terms in small_terms for term in terms])
    flat_small = small_sum(flat_small.reshape(-1, LANES), count).reshape(-1)
    sums, start = [[] for _ in small_terms[0]], 0
    for terms in small_terms:
        for member, term in enumerate(terms):
            sums[member].append(flat_small[start:start + term.shape[0]])
            start += term.shape[0]
    (ln1_gain_sum, ln1_shift_sum, qv_bias_sum, proj_bias_sum, ln2_gain_sum, ln2_shift_sum, fc_bias_sum, out_bias_sum) = [
        jnp.stack(member) for member in sums
    ]
    qv_bias_sum = qv_bias_sum.reshape(layer_count, 2, -1)
    rows = tokens.shape[1] // count
    qkv_sum = jnp.stack([jnp.stack(jnp.split(terms[0], 3, axis=1)) for terms in big_terms])
    proj_sum = jnp.stack([terms[1].T for terms in big_terms])
    fc_sum = jnp.stack([terms[2] for terms in big_terms])
    out_sum = jnp.stack([terms[3].T for terms in big_terms])
    return (
        block_out,
        gradient,
        ln1_gain_sum,
        ln1_shift_sum,
        qkv_sum,
        qv_bias_sum,
        proj_sum,
        proj_bias_sum,
        ln2_gain_sum,
        ln2_shift_sum,
        fc_sum,
        fc_bias_sum,
        out_sum,
        out_bias_sum,
    )


def solution(mesh):
    in_specs = (
        P("dp", None),
        P("dp", None),
        P("dp", None),
        P("dp"),
        P(),
        P(),
        P(None, None, None, "tensor"),
        P(None, None, "tensor"),
        P(None, "tensor", None),
        P(),
        P(),
        P(),
        P(None, None, "tensor"),
        P(None, "tensor"),
        P(None, "tensor", None),
        P(),
    )
    out_specs = (
        P("dp", None),
        P("dp", None),
        P(),
        P(),
        P(None, None, "dp", "tensor"),
        P(None, None, "tensor"),
        P(None, "tensor", "dp"),
        P(),
        P(),
        P(),
        P(None, "dp", "tensor"),
        P(None, "tensor"),
        P(None, "tensor", "dp"),
        P(),
    )
    return jax.shard_map(
        functools.partial(on_device, mesh.shape["dp"], mesh.shape["tensor"]),
        mesh=mesh,
        in_specs=in_specs,
        out_specs=out_specs,
        check_vma=False,
    )
```

time: 1040 us -> 639 us (0.61)
  waiting for transfers between devices: 630 us -> 304 us
  matrix products: 195 us -> 88.9 us
  starting transfers between devices: 1.99 us -> 108 us
  blocking collectives: 81.8 us -> 0 us
  Pallas kernels: 0 us -> 30 us
  local copies, waits for them, and re-layouts: 52.1 us -> 30.8 us
  other arithmetic: 47.4 us -> 64.3 us
  between operations: 17.7 us -> 4.25 us
    reduce_scatter x2 -> x0, waiting for transfers between devices: 328 us -> none  [the longest x1 176 us: on_device(): lax.psum_scatter(fc_view, 'dp', scatter_dimension=2, tiled=True)]
    ppermute x0 -> x108, waiting for transfers between devices: none -> 304 us  [the longest x96 290 us: scatter(): got = lax.ppermute(send, 'dp', [(one, one ^ bit) for one in range(count)])]
    unnamed x11 -> x0, waiting for transfers between devices: 190 us -> none
    psum x7 -> x0, waiting for transfers between devices: 113 us -> none  [the longest x2 40.7 us: on_device(): branch_attn = lax.psum(matmul(attended_flat, proj_float[number]), 'tensor')]
    ppermute x0 -> x108, starting transfers between devices: none -> 108 us  [the longest x96 104 us: scatter(): got = lax.ppermute(send, 'dp', [(one, one ^ bit) for one in range(count)])]
    dot_general x48 -> x60, matrix products: 195 us -> 88.9 us  [the longest x24 28.2 us: weight_product(): lax.dot_general(low, weight, dims, preferred_element_type=F32)]
    psum x1 -> x0, blocking collectives: 81.8 us -> none  [on_device(): lax.psum((stacked_small[0], stacked_small[1], stacked_small[2], stacked_s...]
    pallas_call x0 -> x8, Pallas kernels: none -> 30 us  [grad_parts(): pl.pallas_call(functools.partial(grad_kernel, orders, widths, permuted),...]
  transfers between devices with their start and end apart: 10 -> 108, of which waited for: 9 -> 68; matrix products, arithmetic and copies ran while one was open for 13% -> 20% of each run, Pallas kernels for 0% -> 5%
where the time goes in v1:
time: 639 us; the launch traced here: 630 us
  waiting for transfers between devices  304 us (48%)
  starting transfers between devices  108 us (17%)
  matrix products  88.9 us (14%)
  other arithmetic  64.3 us (10%)
  local copies, waits for them, and re-layouts  30.8 us (5%)
  Pallas kernels  30 us (5%)
    ppermute x96, waiting for transfers between devices, scatter(): got = lax.ppermute(send, 'dp', [(one, one ^ bit) for one in range(count)])  290 us
    ppermute x96, starting transfers between devices, scatter(): got = lax.ppermute(send, 'dp', [(one, one ^ bit) for one in range(count)])  104 us
    pallas_call x8, Pallas kernels, grad_parts(): pl.pallas_call(functools.partial(grad_kernel, orders, widths, permuted),...  30 us
    dot_general x24, matrix products, weight_product(): lax.dot_general(low, weight, dims, preferred_element_type=F32)  28.2 us
    dot_general x24, matrix products, weight_product(): first = lax.dot_general(high, weight, dims, preferred_element_type=F32)  27.4 us
    add x48, other arithmetic, scatter(): keep = keep[:half] + got[:half]  23.5 us
  transfers between devices with their start and end apart: 108, of which 68 were waited for; matrix products, arithmetic and copies ran while one was open for 20% of the time, Pallas kernels for 5%

profile of v1, /device:TPU:0, one launch (start us, length us, event | category | flops | bytes accessed | tf_op | source)
XLA Modules:
  0.0 629.8 jit_solution(18355678535551530767)
XLA Ops:
  46.9 4.8 fusion.25
  69.6 4.6 shard_map.268
  89.3 5.9 collective-permute-done.104
  96.8 4.7 collective-permute-done.81
  108.6 16.0 %collective-permute-done.82 = f32[96,256]{1,0:T(8,128)S(1)} collective-permute-done((f32[96,256]{1,0:T(8,128)S(1)}, f32[96,256]{1,0:T(8,128)S(1)}, u32[]{:S(2)}, u32[]{:S(2)}) %collective-permute-start.82) | collective-permute-done | bytes 98336 | tf_op jit(solution)/shard_map/ppermute | solution.py:193
  198.4 9.6 %collective-permute-done.56 = f32[384,128]{1,0:T(8,128)S(1)} collective-permute-done((f32[384,128]{1,0:T(8,128)S(1)}, f32[384,128]{1,0:T(8,128)S(1)}, u32[]{:S(2)}, u32[]{:S(2)}) %collective-permute-start.56) | collective-permute-done | bytes 196640 | tf_op jit(solution)/shard_map/ppermute | solution.py:193
  208.5 5.2 collective-permute-done.52
  214.6 6.4 %collective-permute-done.48 = f32[384,128]{1,0:T(8,128)S(1)} collective-permute-done((f32[384,128]{1,0:T(8,128)S(1)}, f32[384,128]{1,0:T(8,128)S(1)}, u32[]{:S(2)}, u32[]{:S(2)}) %collective-permute-start.48) | collective-permute-done | bytes 196640 | tf_op jit(solution)/shard_map/ppermute | solution.py:193
  222.3 5.8 collective-permute-done.78
  242.3 5.4 collective-permute-done.103
  256.9 4.6 collective-permute-done.49
  299.5 10.6 %collective-permute-done.34 = f32[96,256]{1,0:T(8,128)S(1)} collective-permute-done((f32[96,256]{1,0:T(8,128)S(1)}, f32[96,256]{1,0:T(8,128)S(1)}, u32[]{:S(2)}, u32[]{:S(2)}) %collective-permute-start.34) | collective-permute-done | bytes 98336 | tf_op jit(solution)/shard_map/ppermute | solution.py:193
  346.2 4.6 shard_map.267
  367.8 6.4 %collective-permute-done.92 = f32[384,256]{1,0:T(8,128)S(1)} collective-permute-done((f32[384,256]{1,0:T(8,128)S(1)}, f32[384,256]{1,0:T(8,128)S(1)}, u32[]{:S(2)}, u32[]{:S(2)}) %collective-permute-start.92) | collective-permute-done | bytes 393248 | tf_op jit(solution)/shard_map/ppermute | solution.py:193
  375.3 9.5 %collective-permute-done.69 = f32[192,256]{1,0:T(8,128)S(1)} collective-permute-done((f32[192,256]{1,0:T(8,128)S(1)}, f32[192,256]{1,0:T(8,128)S(1)}, u32[]{:S(2)}, u32[]{:S(2)}) %collective-permute-start.69) | collective-permute-done | bytes 196640 | tf_op jit(solution)/shard_map/ppermute | solution.py:193
  463.2 10.9 %collective-permute-done.44 = f32[384,128]{1,0:T(8,128)S(1)} collective-permute-done((f32[384,128]{1,0:T(8,128)S(1)}, f32[384,128]{1,0:T(8,128)S(1)}, u32[]{:S(2)}, u32[]{:S(2)}) %collective-permute-start.44) | collective-permute-done | bytes 196640 | tf_op jit(solution)/shard_map/ppermute | solution.py:193
  475.2 4.9 collective-permute-done.40
  481.1 5.0 collective-permute-done.36
  486.9 6.3 %collective-permute-done.66 = f32[96,512]{1,0:T(8,128)S(1)} collective-permute-done((f32[96,512]{1,0:T(8,128)S(1)}, f32[96,512]{1,0:T(8,128)S(1)}, u32[]{:S(2)}, u32[]{:S(2)}) %collective-permute-start.66) | collective-permute-done | bytes 196640 | tf_op jit(solution)/shard_map/ppermute | solution.py:193
  493.9 5.5 collective-permute-done.90
  514.9 5.1 collective-permute-done.67
  520.5 5.6 collective-permute-done.91
  563.5 10.6 %collective-permute-done.22 = f32[96,256]{1,0:T(8,128)S(1)} collective-permute-done((f32[96,256]{1,0:T(8,128)S(1)}, f32[96,256]{1,0:T(8,128)S(1)}, u32[]{:S(2)}, u32[]{:S(2)}) %collective-permute-start.22) | collective-permute-done | bytes 98336 | tf_op jit(solution)/shard_map/ppermute | solution.py:193
  592.3 6.8 %collective-permute-done.63 = f32[48,768]{1,0:T(8,128)S(1)} collective-permute-done((f32[48,768]{1,0:T(8,128)S(1)}, f32[48,768]{1,0:T(8,128)S(1)}, u32[]{:S(2)}, u32[]{:S(2)}) %collective-permute-start.63) | collective-permute-done | bytes 147488 | tf_op jit(solution)/shard_map/ppermute | solution.py:193
  (794 shorter events, 460.6 us)
Async XLA Ops:
  69.4 76.3 %collective-permute-start.4 = (f32[384,768]{1,0:T(8,128)S(1)}, f32[384,768]{1,0:T(8,128)S(1)}, u32[]{:S(2)}, u32[]{:S(2)}) collective-permute-start(f32[384,768]{1,0:T(8,128)S(1)} %fusion.98), channel_id=1, source_target_pairs={{0,1},{1,0},{2,3},{3,2},{4,5},{5,4},{6,7},{7,6},{8,9},{9,8},{10,11... | collective-permute-start | bytes 3538952 | tf_op jit(solution)/shard_map/ppermute | solution.py:31
  85.7 61.6 %collective-permute-start.3 = (f32[384,768]{1,0:T(8,128)S(1)}, f32[384,768]{1,0:T(8,128)S(1)}, u32[]{:S(2)}, u32[]{:S(2)}) collective-permute-start(f32[384,768]{1,0:T(8,128)S(1)} %fusion.101), channel_id=1, source_target_pairs={{0,1},{1,0},{2,3},{3,2},{4,5},{5,4},{6,7},{7,6},{8,9},{9,8},{10,11... | collective-permute-start | bytes 3538952 | tf_op jit(solution)/shard_map/ppermute | solution.py:31
  85.7 55.7 %collective-permute-start.76 = (f32[384,512]{1,0:T(8,128)S(1)}, f32[384,512]{1,0:T(8,128)S(1)}, u32[]{:S(2)}, u32[]{:S(2)}) collective-permute-start(f32[384,512]{1,0:T(8,128)S(1)} %get-tuple-element.95), channel_id=1, source_target_pairs={{0,4},{2,6},{4,0},{6,2},{8,12},{10,14},{12,8},{14,10},{16,20},{18,... | collective-permute-start | bytes 2359304 | tf_op jit(solution)/shard_map/ppermute | solution.py:193
  87.4 55.5 %collective-permute-start.100 = (f32[384,512]{1,0:T(8,128)S(1)}, f32[384,512]{1,0:T(8,128)S(1)}, u32[]{:S(2)}, u32[]{:S(2)}) collective-permute-start(f32[384,512]{1,0:T(8,128)S(1)} %get-tuple-element.107), channel_id=1, source_target_pairs={{0,4},{2,6},{4,0},{6,2},{8,12},{10,14},{12,8},{14,10},{16,20},{18,... | collective-permute-start | bytes 2359304 | tf_op jit(solution)/shard_map/ppermute | solution.py:193
  139.2 41.1 %collective-permute-start.72 = (f32[384,768]{1,0:T(8,128)}, f32[384,768]{1,0:T(8,128)}, u32[]{:S(2)}, u32[]{:S(2)}) collective-permute-start(f32[384,768]{1,0:T(8,128)} %get-tuple-element.93), channel_id=1, source_target_pairs={{0,2},{2,0},{4,6},{6,4},{8,10},{10,8},{12,14},{14,12},{16,18},{18,... | collective-permute-start | bytes 3538952 | tf_op jit(solution)/shard_map/ppermute | solution.py:193
  141.4 52.3 %collective-permute-start.96 = (f32[384,768]{1,0:T(8,128)}, f32[384,768]{1,0:T(8,128)}, u32[]{:S(2)}, u32[]{:S(2)}) collective-permute-start(f32[384,768]{1,0:T(8,128)} %get-tuple-element.105), channel_id=1, source_target_pairs={{0,2},{2,0},{4,6},{6,4},{8,10},{10,8},{12,14},{14,12},{16,18},{18,... | collective-permute-start | bytes 3538952 | tf_op jit(solution)/shard_map/ppermute | solution.py:193
  142.9 41.3 %collective-permute-start.77 = (f32[192,512]{1,0:T(8,128)}, f32[192,512]{1,0:T(8,128)}, u32[]{:S(2)}, u32[]{:S(2)}) collective-permute-start(f32[192,512]{1,0:T(8,128)} %get-tuple-element.179), channel_id=1, source_target_pairs={{0,8},{2,10},{4,12},{6,14},{8,0},{10,2},{12,4},{14,6},{16,24},{18,... | collective-permute-start | bytes 1179656 | tf_op jit(solution)/shard_map/ppermute | solution.py:193
  145.7 51.2 %collective-permute-start.101 = (f32[192,512]{1,0:T(8,128)}, f32[192,512]{1,0:T(8,128)}, u32[]{:S(2)}, u32[]{:S(2)}) collective-permute-start(f32[192,512]{1,0:T(8,128)} %get-tuple-element.175), channel_id=1, source_target_pairs={{0,8},{2,10},{4,12},{6,14},{8,0},{10,2},{12,4},{14,6},{16,24},{18,... | collective-permute-start | bytes 1179656 | tf_op jit(solution)/shard_map/ppermute | solution.py:193
  168.6 164.4 %collective-permute-start.5 = (f32[384,768]{1,0:T(8,128)}, f32[384,768]{1,0:T(8,128)}, u32[]{:S(2)}, u32[]{:S(2)}) collective-permute-start(f32[384,768]{1,0:T(8,128)} %fusion.89), channel_id=1, source_target_pairs={{0,1},{1,0},{2,3},{3,2},{4,5},{5,4},{6,7},{7,6},{8,9},{9,8},{10,11... | collective-permute-start | bytes 3538952 | tf_op jit(solution)/shard_map/ppermute | solution.py:31
  180.3 137.6 %collective-permute-start.24 = (f32[384,512]{1,0:T(8,128)}, f32[384,512]{1,0:T(8,128)}, u32[]{:S(2)}, u32[]{:S(2)}) collective-permute-start(f32[384,512]{1,0:T(8,128)} %get-tuple-element.69), channel_id=1, source_target_pairs={{0,2},{2,0},{4,6},{6,4},{8,10},{10,8},{12,14},{14,12},{16,18},{18,... | collective-permute-start | bytes 2359304 | tf_op jit(solution)/shard_map/ppermute | solution.py:193
  184.2 107.2 %collective-permute-start.28 = (f32[384,384]{1,0:T(8,128)}, f32[384,384]{1,0:T(8,128)}, u32[]{:S(2)}, u32[]{:S(2)}) collective-permute-start(f32[384,384]{1,0:T(8,128)} %get-tuple-element.71), channel_id=1, source_target_pairs={{0,4},{2,6},{4,0},{6,2},{8,12},{10,14},{12,8},{14,10},{16,20},{18,... | collective-permute-start | bytes 1769480 | tf_op jit(solution)/shard_map/ppermute | solution.py:193
  193.7 95.6 %collective-permute-start.32 = (f32[384,256]{1,0:T(8,128)S(1)}, f32[384,256]{1,0:T(8,128)S(1)}, u32[]{:S(2)}, u32[]{:S(2)}) collective-permute-start(f32[384,256]{1,0:T(8,128)S(1)} %copy-done.27), channel_id=1, source_target_pairs={{0,8},{2,10},{4,12},{6,14},{8,0},{10,2},{12,4},{14,6},{16,24},{18,... | collective-permute-start | bytes 1179656 | tf_op jit(solution)/shard_map/ppermute | solution.py:193
  345.0 72.1 %collective-permute-start.6 = (f32[384,768]{1,0:T(8,128)S(1)}, f32[384,768]{1,0:T(8,128)S(1)}, u32[]{:S(2)}, u32[]{:S(2)}) collective-permute-start(f32[384,768]{1,0:T(8,128)S(1)} %fusion.92), channel_id=1, source_target_pairs={{0,1},{1,0},{2,3},{3,2},{4,5},{5,4},{6,7},{7,6},{8,9},{9,8},{10,11... | collective-permute-start | bytes 3538952 | tf_op jit(solution)/shard_map/ppermute | solution.py:31
  351.9 61.1 %collective-permute-start.64 = (f32[384,512]{1,0:T(8,128)S(1)}, f32[384,512]{1,0:T(8,128)S(1)}, u32[]{:S(2)}, u32[]{:S(2)}) collective-permute-start(f32[384,512]{1,0:T(8,128)S(1)} %get-tuple-element.89), channel_id=1, source_target_pairs={{0,4},{2,6},{4,0},{6,2},{8,12},{10,14},{12,8},{14,10},{16,20},{18,... | collective-permute-start | bytes 2359304 | tf_op jit(solution)/shard_map/ppermute | solution.py:193
  352.9 96.8 %collective-permute-start.60 = (f32[384,768]{1,0:T(8,128)}, f32[384,768]{1,0:T(8,128)}, u32[]{:S(2)}, u32[]{:S(2)}) collective-permute-start(f32[384,768]{1,0:T(8,128)} %get-tuple-element.87), channel_id=1, source_target_pairs={{0,2},{2,0},{4,6},{6,4},{8,10},{10,8},{12,14},{14,12},{16,18},{18,... | collective-permute-start | bytes 3538952 | tf_op jit(solution)/shard_map/ppermute | solution.py:193
  366.3 47.9 %collective-permute-start.88 = (f32[384,512]{1,0:T(8,128)S(1)}, f32[384,512]{1,0:T(8,128)S(1)}, u32[]{:S(2)}, u32[]{:S(2)}) collective-permute-start(f32[384,512]{1,0:T(8,128)S(1)} %get-tuple-element.101), channel_id=1, source_target_pairs={{0,4},{2,6},{4,0},{6,2},{8,12},{10,14},{12,8},{14,10},{16,20},{18,... | collective-permute-start | bytes 2359304 | tf_op jit(solution)/shard_map/ppermute | solution.py:193
  411.1 41.9 %collective-permute-start.84 = (f32[384,768]{1,0:T(8,128)}, f32[384,768]{1,0:T(8,128)}, u32[]{:S(2)}, u32[]{:S(2)}) collective-permute-start(f32[384,768]{1,0:T(8,128)} %get-tuple-element.99), channel_id=1, source_target_pairs={{0,2},{2,0},{4,6},{6,4},{8,10},{10,8},{12,14},{14,12},{16,18},{18,... | collective-permute-start | bytes 3538952 | tf_op jit(solution)/shard_map/ppermute | solution.py:193
  414.0 44.9 %collective-permute-start.65 = (f32[192,512]{1,0:T(8,128)}, f32[192,512]{1,0:T(8,128)}, u32[]{:S(2)}, u32[]{:S(2)}) collective-permute-start(f32[192,512]{1,0:T(8,128)} %get-tuple-element.177), channel_id=1, source_target_pairs={{0,8},{2,10},{4,12},{6,14},{8,0},{10,2},{12,4},{14,6},{16,24},{18,... | collective-permute-start | bytes 1179656 | tf_op jit(solution)/shard_map/ppermute | solution.py:193
  415.2 45.4 %collective-permute-start.89 = (f32[192,512]{1,0:T(8,128)}, f32[192,512]{1,0:T(8,128)}, u32[]{:S(2)}, u32[]{:S(2)}) collective-permute-start(f32[192,512]{1,0:T(8,128)} %get-tuple-element.173), channel_id=1, source_target_pairs={{0,8},{2,10},{4,12},{6,14},{8,0},{10,2},{12,4},{14,6},{16,24},{18,... | collective-permute-start | bytes 1179656 | tf_op jit(solution)/shard_map/ppermute | solution.py:193
  438.0 164.9 %collective-permute-start.7 = (f32[384,768]{1,0:T(8,128)}, f32[384,768]{1,0:T(8,128)}, u32[]{:S(2)}, u32[]{:S(2)}) collective-permute-start(f32[384,768]{1,0:T(8,128)} %fusion.91), channel_id=1, source_target_pairs={{0,1},{1,0},{2,3},{3,2},{4,5},{5,4},{6,7},{7,6},{8,9},{9,8},{10,11... | collective-permute-start | bytes 3538952 | tf_op jit(solution)/shard_map/ppermute | solution.py:31
  449.6 132.4 %collective-permute-start.12 = (f32[384,512]{1,0:T(8,128)}, f32[384,512]{1,0:T(8,128)}, u32[]{:S(2)}, u32[]{:S(2)}) collective-permute-start(f32[384,512]{1,0:T(8,128)} %get-tuple-element.63), channel_id=1, source_target_pairs={{0,2},{2,0},{4,6},{6,4},{8,10},{10,8},{12,14},{14,12},{16,18},{18,... | collective-permute-start | bytes 2359304 | tf_op jit(solution)/shard_map/ppermute | solution.py:193
  452.9 102.5 %collective-permute-start.16 = (f32[384,384]{1,0:T(8,128)}, f32[384,384]{1,0:T(8,128)}, u32[]{:S(2)}, u32[]{:S(2)}) collective-permute-start(f32[384,384]{1,0:T(8,128)} %get-tuple-element.65), channel_id=1, source_target_pairs={{0,4},{2,6},{4,0},{6,2},{8,12},{10,14},{12,8},{14,10},{16,20},{18,... | collective-permute-start | bytes 1769480 | tf_op jit(solution)/shard_map/ppermute | solution.py:193
  458.9 95.3 %collective-permute-start.20 = (f32[384,256]{1,0:T(8,128)S(1)}, f32[384,256]{1,0:T(8,128)S(1)}, u32[]{:S(2)}, u32[]{:S(2)}) collective-permute-start(f32[384,256]{1,0:T(8,128)S(1)} %copy-done.25), channel_id=1, source_target_pairs={{0,8},{2,10},{4,12},{6,14},{8,0},{10,2},{12,4},{14,6},{16,24},{18,... | collective-permute-start | bytes 1179656 | tf_op jit(solution)/shard_map/ppermute | solution.py:193
  583.4 27.7 %collective-permute-start.13 = (f32[192,512]{1,0:T(8,128)S(1)}, f32[192,512]{1,0:T(8,128)S(1)}, u32[]{:S(2)}, u32[]{:S(2)}) collective-permute-start(f32[192,512]{1,0:T(8,128)S(1)} %get-tuple-element.181), channel_id=1, source_target_pairs={{0,4},{2,6},{4,0},{6,2},{8,12},{10,14},{12,8},{14,10},{16,20},{18,... | collective-permute-start | bytes 1179656 | tf_op jit(solution)/shard_map/ppermute | solution.py:193
  (235 other events, 1665.5 us)
